TPU v7x, 32 devices: a whole 2x2x4 slice. The times are simulated.
32 devices in a mesh: groups: 2 (over x), pts: 16 (over z, y, core).
Axes of the slice: x: 2, y: 2, z: 4, core: 2. Of those that a mesh axis runs over, the one named last changes fastest.
Arguments:
- points: float32 [64, 131072], P(None, ('groups', 'pts')), parts along dimension 1, may hold values from -16 to 16
- right_side: float32 [16, 131072], P(None, ('groups', 'pts')), parts along dimension 1, may hold values from -24 to 24
- leaf_basis: float32 [512, 64, 256], P(('groups', 'pts')), parts along dimension 0, may hold values from -0.375 to 0.375
- local_transfer: float32 [960, 4096], P(('groups', 'pts')), parts along dimension 0, may hold values from -0.375 to 0.375
- local_skeleton: float32 [448, 4096], P(('groups', 'pts')), parts along dimension 0, may hold values from -16 to 16
- top_transfer: float32 [60, 4096], P('groups'), parts along dimension 0, may hold values from -0.375 to 0.375
- top_skeleton: float32 [60, 4096], P('groups'), parts along dimension 0, may hold values from -16 to 16
- node_slot: int32 [60], P('groups'), parts along dimension 0, may hold values from 0 to 29, each once
- near_leaves: int32 [512, 8], P(('groups', 'pts')), parts along dimension 0, may hold values from -1 to 255, as said below
Outputs:
- solution: float32 [16, 131072], P(None, ('groups', 'pts')), parts along dimension 1
- residual: float32 [16, 131072], P(None, ('groups', 'pts')), parts along dimension 1
There are 2 independent parts, one for each index of `groups`. A program takes and returns all parts, laid end to end along the dimension named above; each array names one. Nothing has to cross between parts.
Inputs may be any that keep to these rules, and one draw needn't show every extreme that they name: `near_leaves`: every listed partner of leaf l is a distinct leaf m with l < m <= l + 16; a leaf's list holds min(8, number of such leaves) partners and -1 in the remaining places, so only the last leaves have padding.
All inputs are finite; a program needn't handle non-finite values.
Results may differ from a plain program's by a relative error of at most 0.0003.
Values sent between devices are 32-bit elements; how exact they have to be, the bound alone decides.
A program may use at most 192 MiB of HBM per device.

v0:
```python
import math

import jax
import jax.numpy as jnp
from jax import lax
from jax.sharding import PartitionSpec as P

ITERS = 3


RIDGE = 8.0
HIGH = lax.Precision.HIGHEST


def passed_along(value, axis, steps):
    count = lax.axis_size(axis)
    first, last = (max(0, -steps), min(count, count - steps))
    return lax.ppermute(value, axis, [(source, source + steps) for source in range(first, last)])


def partner(block, axis, bit):
    count = lax.axis_size(axis)
    route = []
    for low in range(count):
        high = low | 1 << bit
        if high != low and high < count:
            route += [(low, high), (high, low)]
    return lax.ppermute(block, axis, route)


def kernel_block(left, right):
    features = left.shape[-2]
    left_sq = jnp.sum(left * left, axis=-2)[..., :, None]
    right_sq = jnp.sum(right * right, axis=-2)[..., None, :]
    cross = jnp.einsum("...dn,...dm->...nm", left, right, precision=HIGH)
    return jnp.exp((2.0 * cross - left_sq - right_sq) / (2.0 * features))


def couple_pairs(blocks, charges):
    pairs = blocks.shape[0]
    paired = charges.reshape(pairs, 2, charges.shape[1], charges.shape[2])
    first = jnp.einsum("prs,pns->pnr", blocks, paired[:, 1], precision=HIGH)
    second = jnp.einsum("prs,pnr->pns", blocks, paired[:, 0], precision=HIGH)
    return jnp.stack([first, second], axis=1).reshape(charges.shape)


def lift_charges(charges, transfer):
    lifted = jnp.einsum("jnc,jcp->jnp", charges, transfer, precision=HIGH)
    return lifted.reshape(-1, 2, lifted.shape[1], lifted.shape[2]).sum(axis=1)


def lower_potential(potential, transfer):
    return jnp.einsum("jnp,jcp->jnc", jnp.repeat(potential, 2, axis=0), transfer, precision=HIGH)


def inner_product(first, second):
    return jnp.sum(first * second, axis=1)


def per_device(
    points,
    right_side,
    leaf_basis,
    local_transfer,
    local_skeleton,
    top_transfer,
    top_skeleton,
    node_slot,
    near_leaves,
):
    features = points.shape[0]
    leaves, skeleton_rank, leaf_size = leaf_basis.shape
    columns = right_side.shape[0]
    low_depths = leaves.bit_length() - 1
    devices = lax.axis_size("pts")
    top_depths = devices.bit_length() - 1
    position = lax.axis_index("pts")
    coupling = 1.0 / math.sqrt(skeleton_rank)
    near_scale = 1.0 / math.sqrt(leaf_size)
    own_points = points.reshape(features, leaves, leaf_size).transpose(1, 0, 2)
    next_points = passed_along(points, "pts", -1)
    next_points = next_points.reshape(features, leaves, leaf_size).transpose(1, 0, 2)
    joined_points = jnp.concatenate([own_points, next_points], axis=0)
    present = near_leaves >= 0
    partner_index = jnp.where(present, near_leaves - position * leaves, 0)
    weights = present.astype(jnp.float32)
    self_blocks = kernel_block(own_points, own_points) * near_scale
    cross_blocks = kernel_block(own_points[:, None], joined_points[partner_index]) * near_scale
    spread = (partner_index[..., None] == jnp.arange(2 * leaves, dtype=jnp.int32)).astype(
        jnp.float32
    ) * weights[..., None]
    lower_e = local_transfer.reshape(2 * leaves - 2, skeleton_rank, skeleton_rank)
    lower_s = local_skeleton.reshape(leaves - 2, features, skeleton_rank)
    transfers = []
    pair_blocks = [None]
    for depth in range(low_depths):
        node_count = leaves >> depth
        offset = 2 * leaves - 2 * node_count
        transfers.append(lower_e[offset : offset + node_count])
        if depth > 0:
            first_row = leaves - (leaves >> depth - 1)
            skeletons = lower_s[first_row : first_row + node_count].reshape(
                node_count // 2, 2, features, skeleton_rank
            )
            pair_blocks.append(kernel_block(skeletons[:, 0], skeletons[:, 1]) * coupling)
    own_e, sibling_e, chain_blocks = ([], [], [])
    for depth in range(top_depths):
        offset = 2 * devices - 2 * (devices >> depth)
        subtree = jnp.right_shift(position, depth)
        own_slot = node_slot[offset + subtree]
        sibling_slot = node_slot[offset + jnp.bitwise_xor(subtree, 1)]
        own_e.append(top_transfer[own_slot].reshape(skeleton_rank, skeleton_rank))
        sibling_e.append(top_transfer[sibling_slot].reshape(skeleton_rank, skeleton_rank))
        own_skeleton = top_skeleton[own_slot].reshape(features, skeleton_rank)
        sibling_skeleton = top_skeleton[sibling_slot].reshape(features, skeleton_rank)
        chain_blocks.append(kernel_block(own_skeleton, sibling_skeleton) * coupling)

    def upper_pass(root_charge):
        pending = []
        charge = root_charge
        for depth in range(top_depths):
            sibling = partner(charge, "pts", depth)
            pending.append(jnp.einsum("rs,ns->nr", chain_blocks[depth], sibling, precision=HIGH))
            if depth + 1 < top_depths:
                charge = jnp.dot(charge, own_e[depth], precision=HIGH) + jnp.dot(
                    sibling, sibling_e[depth], precision=HIGH
                )
        potential = pending[-1]
        for depth in range(top_depths - 2, -1, -1):
            potential = (
                jnp.einsum("np,cp->nc", potential, own_e[depth], precision=HIGH) + pending[depth]
            )
        return potential

    def operate(vec):
        blocks = vec.reshape(columns, leaves, leaf_size)
        following = passed_along(vec, "pts", -1).reshape(columns, leaves, leaf_size)
        joined_values = jnp.concatenate([blocks, following], axis=1)
        partner_values = joined_values[:, partner_index] * weights[None, :, :, None]
        local_term = jnp.einsum("lim,nlm->nli", self_blocks, blocks, precision=HIGH)
        local_term = local_term + jnp.einsum(
            "lkim,nlkm->nli", cross_blocks, partner_values, precision=HIGH
        )
        sent = jnp.einsum("lkim,nli->nlkm", cross_blocks, blocks, precision=HIGH)
        spread_back = jnp.einsum("lke,nlkm->nem", spread, sent, precision=HIGH)
        incoming = passed_along(spread_back[:, leaves:], "pts", 1)
        near_term = local_term + spread_back[:, :leaves] + incoming
        charges = [jnp.einsum("lrp,nlp->lnr", leaf_basis, blocks, precision=HIGH)]
        for depth in range(low_depths):
            charges.append(lift_charges(charges[-1], transfers[depth]))
        potential = upper_pass(charges[-1][0])[None]
        for depth in range(low_depths - 1, -1, -1):
            potential = lower_potential(potential, transfers[depth])
            if depth > 0:
                potential = potential + couple_pairs(pair_blocks[depth], charges[depth])
        far_term = jnp.einsum("lrp,lnr->nlp", leaf_basis, potential, precision=HIGH)
        return RIDGE * vec + (near_term + far_term).reshape(columns, leaves * leaf_size)

    solution = jnp.zeros_like(right_side)
    residual = right_side

    def joined_sums(vec, image):
        return lax.psum((inner_product(vec, vec), inner_product(vec, image)), "pts")

    image = operate(residual)
    norm_now, product = joined_sums(residual, image)
    step_length = norm_now / product
    direction, along = (residual, image)
    for sweep in range(ITERS):
        solution = solution + step_length[:, None] * direction
        residual = residual - step_length[:, None] * along
        if sweep + 1 < ITERS:
            image = operate(residual)
            norm_next, product = joined_sums(residual, image)
            ratio = norm_next / norm_now
            step_length = norm_next / (product - ratio * norm_next / step_length)
            direction = residual + ratio[:, None] * direction
            along = image + ratio[:, None] * along
            norm_now = norm_next
    return (solution, residual)


def solution(mesh):
    return jax.shard_map(
        per_device,
        mesh=mesh,
        in_specs=(
            P(None, ("groups", "pts")),
            P(None, ("groups", "pts")),
            P(("groups", "pts"), None, None),
            P(("groups", "pts"), None),
            P(("groups", "pts"), None),
            P("groups", None),
            P("groups", None),
            P("groups"),
            P(("groups", "pts"), None),
        ),
        out_specs=(P(None, ("groups", "pts")), P(None, ("groups", "pts"))),
        check_vma=False,
    )
```

profile of v0, /device:TPU:0, one launch (start us, length us, event | category | flops | bytes accessed | tf_op | source)
XLA Modules:
  0.0 522.7 jit_solution(8545079541798553838)
XLA Ops:
  0.7 1.4 collective-permute-start
  6.4 1.9 fusion.154
  11.4 1.6 collective-permute-start.1
  29.9 1.6 slice.147
  33.2 1.7 copy.153
  43.2 2.8 dynamic-slice_reduce_fusion
  51.5 1.4 fusion.159
  54.5 6.1 %exponential_multiply_fusion.1 = f32[16,256,256]{2,1,0:T(8,128)} fusion(f32[16,256]{1,0:T(8,128)S(1)} %multiply_reduce_fusion.1, f32[8,16,8,256]{3,2,1,0:T(8,128)S(1)} %bitcast.606), kind=kOutput, calls=%fused_computation.20 | convolution fusion | flops 810549248 | bytes 5259264 | tf_op jit(solution)/shard_map/...dn,...dm->...nm/dot_general | solution.py:35
  73.8 3.6 collective-permute-start.4
  77.6 1.5 collective-permute-done.4
  80.0 3.2 collective-permute-start.5
  83.3 1.5 collective-permute-done.5
  84.8 1.5 convolution_add_fusion.26
  86.3 3.0 collective-permute-start.6
  92.6 1.5 copy.92
  105.8 2.1 gather_fusion
  109.2 1.4 pad_maximum_fusion
  110.7 4.3 gather_fusion.1
  115.0 5.0 multiply_reduce_fusion
  120.7 43.1 %exponential_multiply_fusion = f32[16,8,256,256]{3,2,1,0:T(8,128)} fusion(f32[16,8,256]{2,1,0:T(8,128)S(1)} %multiply_reduce_fusion, f32[16,256]{1,0:T(8,128)S(1)} %copy-done.84, f32[16,8,64,256]{3,2,1,0:T(8,128)S(1)} %bitcast.588, f32[8,16,8,256]{3,2,1,0:T(8,128)} %bitcast.604), kind=kOutput, calls=%fused_computation.18 | convolution fusion | flops 6484393984 | bytes 43139072 | tf_op jit(solution)/shard_map/...dn,...dm->...nm/dot_general | solution.py:35
  163.8 32.3 %fusion.26 = f32[16,16,8,256]{3,0,2,1:T(8,128)S(1)} fusion(f32[16,8,256,256]{3,2,1,0:T(8,128)} %exponential_multiply_fusion, f32[16,16,256,1]{2,1,0,3:T(8,128)} %bitcast.623), kind=kOutput, calls=%fused_computation.34 | convolution fusion | flops 1610612736 | bytes 35913728 | tf_op jit(solution)/shard_map/lkim,nli->nlkm/dot_general | solution.py:144
  196.1 3.1 fusion.35
  200.3 2.0 collective-permute-start.2
  202.3 21.0 %fusion.44 = f32[16,16,256]{2,0,1:T(8,128)S(1)} fusion(f32[16,8,256,256]{3,2,1,0:T(8,128)} %exponential_multiply_fusion, f32[16,8,16,256]{3,2,1,0:T(8,128)} %bitcast.601, f32[16,8]{1,0:T(8,128)S(1)} %copy.75), kind=kOutput, calls=%fused_computation.40 | convolution fusion | flops 1611137024 | bytes 35914240 | tf_op jit(solution)/shard_map/lkim,nlkm->nli/dot_general | solution.py:141
  223.4 6.0 %fusion.69 = f32[16,2,8,256]{3,2,1,0:T(8,128)S(1)} fusion(f32[16,16,256]{2,0,1:T(8,128)} %convolution_bitcast_fusion.3, f32[16,16,256]{2,0,1:T(8,128)} %collective-permute-done.2, f32[16,16,256]{2,0,1:T(8,128)S(1)} %fusion.44, f32[16,256,256]{2,1,0:T(8,128)} %exponential_multiply_fusion.1, f32[16,32,256]{2,0,1:T(8,128)S(1)} %bitcast.622, ...), kind=kOutput, calls=%fused_computation.59 | convolution fusion | flops 201588736 | bytes 5767168 | tf_op jit(solution)/shard_map/lim,nlm->nli/dot_general | solution.py:140
  229.6 31.0 %all-reduce.2 = (f32[16]{0:T(128)S(1)}, f32[16]{0:T(128)S(1)}) all-reduce(f32[16]{0:T(128)S(1)} %get-tuple-element.21, f32[16]{0:T(128)S(1)} %get-tuple-element.20), channel_id=1, replica_groups=mesh['groups'=2,'pts'=16] {'pts'}, use_global_device_ids=true, to_apply=%region_1.2 | all-reduce | flops 32 | bytes 256 | tf_op jit(solution)/shard_map/psum | solution.py:163
  266.8 1.4 fusion.167
  271.7 32.4 %fusion.29 = f32[16,16,8,256]{3,0,2,1:T(8,128)} fusion(f32[16,8,256,256]{3,2,1,0:T(8,128)} %exponential_multiply_fusion, f32[16,16,256,1]{2,1,0,3:T(8,128)S(1)} %bitcast.624), kind=kOutput, calls=%fused_computation.35 | convolution fusion | flops 1610612736 | bytes 35913728 | tf_op jit(solution)/shard_map/lkim,nli->nlkm/dot_general | solution.py:144
  304.3 4.1 fusion.38
  309.5 2.6 collective-permute-start.8
  313.5 3.5 collective-permute-done.10
  317.2 3.5 collective-permute-done.11
  321.0 4.5 collective-permute-done.12
  331.8 2.1 gather_fusion.2
  333.9 20.9 %fusion.49 = f32[16,16,256]{2,1,0:T(8,128)} fusion(f32[16,8,256,256]{3,2,1,0:T(8,128)} %exponential_multiply_fusion, f32[16,8,16,256]{3,2,1,0:T(8,128)} %bitcast.603, f32[16,8]{1,0:T(8,128)S(1)} %copy.75), kind=kOutput, calls=%fused_computation.41 | convolution fusion | flops 1611137024 | bytes 35914240 | tf_op jit(solution)/shard_map/lkim,nlkm->nli/dot_general | solution.py:141
  354.8 5.9 %fusion.71 = f32[16,2,8,256]{3,2,1,0:T(8,128)S(1)} fusion(f32[16,16,256]{2,0,1:T(8,128)} %convolution_bitcast_fusion.2, f32[16,16,256]{2,0,1:T(8,128)} %collective-permute-done.8, f32[16,16,256]{2,1,0:T(8,128)} %fusion.49, f32[16,256,256]{2,1,0:T(8,128)} %exponential_multiply_fusion.1, f32[16,32,256]{2,0,1:T(8,128)S(1)} %bitcast.620, ...), kind=kOutput, calls=%fused_computation.61 | convolution fusion | flops 201588736 | bytes 5767168 | tf_op jit(solution)/shard_map/lim,nlm->nli/dot_general | solution.py:140
  360.9 29.5 %all-reduce.1 = (f32[16]{0:T(128)S(1)}, f32[16]{0:T(128)S(1)}) all-reduce(f32[16]{0:T(128)S(1)} %get-tuple-element.19, f32[16]{0:T(128)S(1)} %get-tuple-element.18), channel_id=1, replica_groups=mesh['groups'=2,'pts'=16] {'pts'}, use_global_device_ids=true, to_apply=%region_24.25 | all-reduce | flops 32 | bytes 256 | tf_op jit(solution)/shard_map/psum | solution.py:163
  398.4 1.5 fusion.175
  402.8 32.2 %fusion.32 = f32[16,16,8,256]{3,0,2,1:T(8,128)} fusion(f32[16,8,256,256]{3,2,1,0:T(8,128)} %exponential_multiply_fusion, f32[16,16,256,1]{2,1,0,3:T(8,128)S(1)} %bitcast.625), kind=kOutput, calls=%fused_computation.36 | convolution fusion | flops 1610612736 | bytes 35913728 | tf_op jit(solution)/shard_map/lkim,nli->nlkm/dot_general | solution.py:144
  435.2 4.0 fusion.41
  440.3 2.6 collective-permute-start.14
  445.8 2.7 collective-permute-done.16
  448.8 3.5 collective-permute-done.17
  452.5 4.5 collective-permute-done.18
  462.6 2.1 gather_fusion.3
  464.7 21.1 %fusion.54 = f32[16,16,256]{2,1,0:T(8,128)S(1)} fusion(f32[16,8,256,256]{3,2,1,0:T(8,128)} %exponential_multiply_fusion, f32[16,8,16,256]{3,2,1,0:T(8,128)} %bitcast.602, f32[16,8]{1,0:T(8,128)S(1)} %copy.75), kind=kOutput, calls=%fused_computation.42 | convolution fusion | flops 1611137024 | bytes 35914240 | tf_op jit(solution)/shard_map/lkim,nlkm->nli/dot_general | solution.py:141
  485.9 5.8 %fusion.73 = f32[16,2,8,256]{3,2,1,0:T(8,128)S(1)} fusion(f32[16,16,256]{2,0,1:T(8,128)S(1)} %convolution_bitcast_fusion.1, f32[16,16,256]{2,0,1:T(8,128)} %collective-permute-done.14, f32[16,16,256]{2,1,0:T(8,128)S(1)} %fusion.54, f32[16,256,256]{2,1,0:T(8,128)} %exponential_multiply_fusion.1, f32[16,32,256]{2,0,1:T(8,128)S(1)} %bitcast.618, ...), kind=kOutput, calls=%fused_computation.63 | convolution fusion | flops 201588736 | bytes 5767168 | tf_op jit(solution)/shard_map/lim,nlm->nli/dot_general | solution.py:140
  491.9 29.5 %all-reduce = (f32[16]{0:T(128)S(1)}, f32[16]{0:T(128)S(1)}) all-reduce(f32[16]{0:T(128)S(1)} %get-tuple-element.17, f32[16]{0:T(128)S(1)} %get-tuple-element.16), channel_id=1, replica_groups=mesh['groups'=2,'pts'=16] {'pts'}, use_global_device_ids=true, to_apply=%region_31.32 | all-reduce | flops 32 | bytes 256 | tf_op jit(solution)/shard_map/psum | solution.py:163
  (424 shorter events, 99.3 us)
Async XLA Ops:
  0.7 104.0 %collective-permute-start = (f32[16,4096]{1,0:T(8,128)}, f32[16,4096]{1,0:T(8,128)}, u32[]{:S(2)}, u32[]{:S(2)}) collective-permute-start(f32[16,4096]{1,0:T(8,128)} %param.10), channel_id=1, source_target_pairs={{1,0},{2,1},{3,2},{4,3},{5,4},{6,5},{7,6},{8,7},{9,8},{10,9},{11,1... | collective-permute-start | bytes 786440 | tf_op jit(solution)/shard_map/ppermute | solution.py:18
  6.1 96.4 %copy-start.2 = (f32[16,64,64]{2,1,0:T(8,128)}, f32[16,64,64]{2,1,0:T(8,128)S(1)}, u32[]{:S(2)}) copy-start(f32[16,64,64]{2,1,0:T(8,128)S(1)} %slice.129) | copy-start | bytes 786436
  6.2 94.9 %copy-start.5 = (f32[8,64,64]{2,1,0:T(8,128)}, f32[8,64,64]{2,1,0:T(8,128)S(1)}, u32[]{:S(2)}) copy-start(f32[8,64,64]{2,1,0:T(8,128)S(1)} %slice.131) | copy-start | bytes 393220
  6.4 92.6 %copy-start.12 = (f32[2,64,64]{2,1,0:T(8,128)}, f32[2,64,64]{2,1,0:T(8,128)S(1)}, u32[]{:S(2)}) copy-start(f32[2,64,64]{2,1,0:T(8,128)S(1)} %slice.135) | copy-start | bytes 98308
  6.4 46.6 %copy-start.85 = (s32[16,8]{0,1:T(8,128)S(1)}, s32[16,8]{0,1:T(8,128)}, u32[]{:S(2)}) copy-start(s32[16,8]{0,1:T(8,128)} %param.17) | copy-start | bytes 1540
  10.3 62.6 %collective-permute-start.3 = (f32[16,64]{1,0:T(8,128)}, f32[16,64]{1,0:T(8,128)S(1)}, u32[]{:S(2)}, u32[]{:S(2)}) collective-permute-start(f32[16,64]{1,0:T(8,128)} %convolution_bitcast_fusion.24), channel_id=1, source_target_pairs={{0,1},{1,0},{2,3},{3,2},{4,5},{5,4},{6,7},{7,6},{8,9},{9,8},{10,11... | collective-permute-start | bytes 12296 | tf_op jit(solution)/shard_map/ppermute | solution.py:28
  11.4 96.4 %collective-permute-start.1 = (f32[64,4096]{1,0:T(8,128)S(1)}, f32[64,4096]{1,0:T(8,128)}, u32[]{:S(2)}, u32[]{:S(2)}) collective-permute-start(f32[64,4096]{1,0:T(8,128)S(1)} %copy-done.9), channel_id=1, source_target_pairs={{1,0},{2,1},{3,2},{4,3},{5,4},{6,5},{7,6},{8,7},{9,8},{10,9},{11,1... | collective-permute-start | bytes 3145736 | tf_op jit(solution)/shard_map/ppermute | solution.py:18
  36.4 24.1 %copy-start.7 = (f32[4,64,64]{2,1,0:T(8,128)}, f32[4,64,64]{2,1,0:T(8,128)S(1)}, u32[]{:S(2)}) copy-start(f32[4,64,64]{2,1,0:T(8,128)S(1)} %fusion.77) | copy-start | bytes 196612
  51.5 46.5 %copy-start.21 = (f32[64,64]{1,0:T(8,128)}, f32[64,64]{1,0:T(8,128)S(1)}, u32[]{:S(2)}) copy-start(f32[64,64]{1,0:T(8,128)S(1)} %reshape_squeeze.42) | copy-start | bytes 49156
  54.5 36.0 %copy-start.4 = (f32[16,4096]{1,0:T(8,128)S(1)}, f32[16,4096]{1,0:T(8,128)}, u32[]{:S(2)}) copy-start(f32[16,4096]{1,0:T(8,128)} %param.10) | copy-start | bytes 786436
  61.4 36.7 %copy-start.35 = (f32[64,64]{1,0:T(8,128)S(1)}, f32[64,64]{1,0:T(8,128)}, u32[]{:S(2)}) copy-start(f32[64,64]{1,0:T(8,128)} %fusion.93) | copy-start | bytes 49156
  61.7 44.0 %copy-start.38 = (f32[64,64]{1,0:T(8,128)}, f32[64,64]{1,0:T(8,128)S(1)}, u32[]{:S(2)}) copy-start(f32[64,64]{1,0:T(8,128)S(1)} %fusion.98) | copy-start | bytes 49156
  62.0 43.7 %copy-start.41 = (f32[64,64]{1,0:T(8,128)}, f32[64,64]{1,0:T(8,128)S(1)}, u32[]{:S(2)}) copy-start(f32[64,64]{1,0:T(8,128)S(1)} %fusion.103) | copy-start | bytes 49156
  67.8 37.9 %copy-start.25 = (f32[64,64]{1,0:T(8,128)}, f32[64,64]{1,0:T(8,128)S(1)}, u32[]{:S(2)}) copy-start(f32[64,64]{1,0:T(8,128)S(1)} %reshape_squeeze.44) | copy-start | bytes 49156
  70.0 35.7 %copy-start.28 = (f32[64,64]{1,0:T(8,128)}, f32[64,64]{1,0:T(8,128)S(1)}, u32[]{:S(2)}) copy-start(f32[64,64]{1,0:T(8,128)S(1)} %reshape_squeeze.46) | copy-start | bytes 49156
  73.8 5.3 %collective-permute-start.4 = (f32[16,64]{1,0:T(8,128)S(1)}, f32[16,64]{1,0:T(8,128)S(1)}, u32[]{:S(2)}, u32[]{:S(2)}) collective-permute-start(f32[16,64]{1,0:T(8,128)S(1)} %convolution_add_fusion.28), channel_id=1, source_target_pairs={{0,2},{2,0},{1,3},{3,1},{4,6},{6,4},{5,7},{7,5},{8,10},{10,8},{9,1... | collective-permute-start | bytes 12296 | tf_op jit(solution)/shard_map/ppermute | solution.py:28
  80.0 4.8 collective-permute-start.5
  86.3 8.6 %collective-permute-start.6 = (f32[16,64]{1,0:T(8,128)}, f32[16,64]{1,0:T(8,128)}, u32[]{:S(2)}, u32[]{:S(2)}) collective-permute-start(f32[16,64]{1,0:T(8,128)} %convolution_add_fusion.26), channel_id=1, source_target_pairs={{0,8},{8,0},{1,9},{9,1},{2,10},{10,2},{3,11},{11,3},{4,12},{12,4},... | collective-permute-start | bytes 12296 | tf_op jit(solution)/shard_map/ppermute | solution.py:28
  200.3 23.1 %collective-permute-start.2 = (f32[16,16,256]{2,0,1:T(8,128)}, f32[16,16,256]{2,0,1:T(8,128)}, u32[]{:S(2)}, u32[]{:S(2)}) collective-permute-start(f32[16,16,256]{2,0,1:T(8,128)} %slice.176), channel_id=1, source_target_pairs={{0,1},{1,2},{2,3},{3,4},{4,5},{5,6},{6,7},{7,8},{8,9},{9,10},{10,1... | collective-permute-start | bytes 786440 | tf_op jit(solution)/shard_map/ppermute | solution.py:18
  223.4 40.3 %copy-start.3 = (f32[16,64,64]{2,1,0:T(8,128)S(1)}, f32[16,64,64]{2,1,0:T(8,128)}, u32[]{:S(2)}) copy-start(f32[16,64,64]{2,1,0:T(8,128)} %copy-done.2) | copy-start | bytes 786436
  223.4 40.9 %copy-start.6 = (f32[8,64,64]{2,1,0:T(8,128)S(1)}, f32[8,64,64]{2,1,0:T(8,128)}, u32[]{:S(2)}) copy-start(f32[8,64,64]{2,1,0:T(8,128)} %copy-done.5) | copy-start | bytes 393220
  223.4 41.5 %copy-start.13 = (f32[2,64,64]{2,1,0:T(8,128)S(1)}, f32[2,64,64]{2,1,0:T(8,128)}, u32[]{:S(2)}) copy-start(f32[2,64,64]{2,1,0:T(8,128)} %copy-done.12) | copy-start | bytes 98308
  223.4 43.4 %copy-start.22 = (f32[64,64]{1,0:T(8,128)S(1)}, f32[64,64]{1,0:T(8,128)}, u32[]{:S(2)}) copy-start(f32[64,64]{1,0:T(8,128)} %copy-done.21) | copy-start | bytes 49156
  223.4 44.9 %copy-start.11 = (f32[2,64,64]{2,1,0:T(8,128)S(1)}, f32[2,64,64]{2,1,0:T(8,128)}, u32[]{:S(2)}) copy-start(f32[2,64,64]{2,1,0:T(8,128)} %copy-done.10) | copy-start | bytes 98308
  223.4 46.4 %copy-start.8 = (f32[4,64,64]{2,1,0:T(8,128)S(1)}, f32[4,64,64]{2,1,0:T(8,128)}, u32[]{:S(2)}) copy-start(f32[4,64,64]{2,1,0:T(8,128)} %copy-done.7) | copy-start | bytes 196612
  260.7 70.0 %collective-permute-start.7 = (f32[16,4096]{1,0:T(8,128)S(1)}, f32[16,4096]{1,0:T(8,128)}, u32[]{:S(2)}, u32[]{:S(2)}) collective-permute-start(f32[16,4096]{1,0:T(8,128)S(1)} %multiply_subtract_fusion.2), channel_id=1, source_target_pairs={{1,0},{2,1},{3,2},{4,3},{5,4},{6,5},{7,6},{8,7},{9,8},{10,9},{11,1... | collective-permute-start | bytes 786440 | tf_op jit(solution)/shard_map/ppermute | solution.py:18
  265.7 46.7 %collective-permute-start.9 = (f32[16,64]{1,0:T(8,128)}, f32[16,64]{1,0:T(8,128)}, u32[]{:S(2)}, u32[]{:S(2)}) collective-permute-start(f32[16,64]{1,0:T(8,128)} %convolution_bitcast_fusion.21), channel_id=1, source_target_pairs={{0,1},{1,0},{2,3},{3,2},{4,5},{5,4},{6,7},{7,6},{8,9},{9,8},{10,11... | collective-permute-start | bytes 12296 | tf_op jit(solution)/shard_map/ppermute | solution.py:28
  304.3 27.5 %copy-start.33 = (f32[2,16,8,256]{3,2,0,1:T(8,128)S(1)}, f32[2,16,8,256]{3,2,0,1:T(8,128)}, u32[]{:S(2)}) copy-start(f32[2,16,8,256]{3,2,0,1:T(8,128)} %copy.228) | copy-start | bytes 786436
  308.7 23.1 %copy-start.16 = (f32[16,256,32]{1,0,2:T(8,128)}, f32[16,256,32]{1,0,2:T(8,128)S(1)}, u32[]{:S(2)}) copy-start(f32[16,256,32]{1,0,2:T(8,128)S(1)} %copy.223) | copy-start | bytes 1572868
  309.5 45.3 %collective-permute-start.8 = (f32[16,16,256]{2,0,1:T(8,128)}, f32[16,16,256]{2,0,1:T(8,128)}, u32[]{:S(2)}, u32[]{:S(2)}) collective-permute-start(f32[16,16,256]{2,0,1:T(8,128)} %slice.190), channel_id=1, source_target_pairs={{0,1},{1,2},{2,3},{3,4},{4,5},{5,6},{6,7},{7,8},{8,9},{9,10},{10,1... | collective-permute-start | bytes 786440 | tf_op jit(solution)/shard_map/ppermute | solution.py:18
  313.3 3.7 collective-permute-start.10
  317.1 3.7 collective-permute-start.11
  320.9 4.6 collective-permute-start.12
  392.4 69.2 %collective-permute-start.13 = (f32[16,4096]{1,0:T(8,128)S(1)}, f32[16,4096]{1,0:T(8,128)}, u32[]{:S(2)}, u32[]{:S(2)}) collective-permute-start(f32[16,4096]{1,0:T(8,128)S(1)} %get-tuple-element.32), channel_id=1, source_target_pairs={{1,0},{2,1},{3,2},{4,3},{5,4},{6,5},{7,6},{8,7},{9,8},{10,9},{11,1... | collective-permute-start | bytes 786440 | tf_op jit(solution)/shard_map/ppermute | solution.py:18
  396.5 46.4 %copy-start.66 = (f32[2,16,64]{2,1,0:T(8,128)}, f32[2,16,64]{2,1,0:T(8,128)S(1)}, u32[]{:S(2)}) copy-start(f32[2,16,64]{2,1,0:T(8,128)S(1)} %bitcast_reduce_fusion.6) | copy-start | bytes 24580
  397.3 46.6 %collective-permute-start.15 = (f32[16,64]{1,0:T(8,128)}, f32[16,64]{1,0:T(8,128)}, u32[]{:S(2)}, u32[]{:S(2)}) collective-permute-start(f32[16,64]{1,0:T(8,128)} %convolution_bitcast_fusion.18), channel_id=1, source_target_pairs={{0,1},{1,0},{2,3},{3,2},{4,5},{5,4},{6,7},{7,6},{8,9},{9,8},{10,11... | collective-permute-start | bytes 12296 | tf_op jit(solution)/shard_map/ppermute | solution.py:28
  402.8 32.2 %copy-start.72 = (s32[16,8]{0,1:T(8,128)S(1)}, s32[16,8]{0,1:T(8,128)}, u32[]{:S(2)}) copy-start(s32[16,8]{0,1:T(8,128)} %get-tuple-element.38) | copy-start | bytes 1540
  435.2 27.4 %copy-start.32 = (f32[2,16,8,256]{3,2,0,1:T(8,128)S(1)}, f32[2,16,8,256]{3,2,0,1:T(8,128)}, u32[]{:S(2)}) copy-start(f32[2,16,8,256]{3,2,0,1:T(8,128)} %copy.226) | copy-start | bytes 786436
  440.3 45.6 %collective-permute-start.14 = (f32[16,16,256]{2,0,1:T(8,128)}, f32[16,16,256]{2,0,1:T(8,128)}, u32[]{:S(2)}, u32[]{:S(2)}) collective-permute-start(f32[16,16,256]{2,0,1:T(8,128)} %slice.198), channel_id=1, source_target_pairs={{0,1},{1,2},{2,3},{3,4},{4,5},{5,6},{6,7},{7,8},{8,9},{9,10},{10,1... | collective-permute-start | bytes 786440 | tf_op jit(solution)/shard_map/ppermute | solution.py:18
  444.8 3.7 collective-permute-start.16
  448.6 3.7 collective-permute-start.17
  452.4 4.6 collective-permute-start.18
  485.8 35.5 %copy-start.99 = (f32[16]{0:T(128)S(1)}, f32[16]{0:T(128)}, u32[]{:S(2)}) copy-start(f32[16]{0:T(128)} %copy-done.98) | copy-start | bytes 196
  485.8 35.5 %copy-start.100 = (f32[16]{0:T(128)S(1)}, f32[16]{0:T(128)}, u32[]{:S(2)}) copy-start(f32[16]{0:T(128)} %get-tuple-element.35) | copy-start | bytes 196
  485.8 35.5 %copy-start.31 = (f32[16,4096]{1,0:T(8,128)S(1)}, f32[16,4096]{1,0:T(8,128)}, u32[]{:S(2)}) copy-start(f32[16,4096]{1,0:T(8,128)} %get-tuple-element.33) | copy-start | bytes 786436
  485.8 35.5 %copy-start.87 = (f32[16]{0:T(128)S(1)}, f32[16]{0:T(128)}, u32[]{:S(2)}) copy-start(f32[16]{0:T(128)} %copy-done.86) | copy-start | bytes 196
  485.9 35.5 %copy-start.89 = (f32[16]{0:T(128)S(1)}, f32[16]{0:T(128)}, u32[]{:S(2)}) copy-start(f32[16]{0:T(128)} %copy-done.88) | copy-start | bytes 196
  485.9 35.5 %copy-start.102 = (f32[16]{0:T(128)S(1)}, f32[16]{0:T(128)}, u32[]{:S(2)}) copy-start(f32[16]{0:T(128)} %copy-done.101) | copy-start | bytes 196
  (76 other events, 846.3 us)
where the time goes:
time: 528 us; the launch traced here: 523 us
  matrix products  293 us (55%)
  blocking collectives  89.9 us (17%)
  local copies, waits for them, and re-layouts  49.3 us (9%)
  starting transfers between devices  26.9 us (5%)
  waiting for transfers between devices  25.2 us (5%)
  other arithmetic  20.5 us (4%)
  between operations  17.9 us (3%)
    dot_general x3, matrix products, operate(): sent = jnp.einsum('lkim,nli->nlkm', cross_blocks, blocks, precision=HIGH)  97 us
    psum x3, blocking collectives, joined_sums(): return lax.psum((inner_product(vec, vec), inner_product(vec, image)), 'pts')  89.9 us
    dot_general x3, matrix products, operate(): jnp.einsum('lkim,nlkm->nli', cross_blocks, partner_values, precision=HIGH)  63 us
    dot_general x9, matrix products, kernel_block(): cross = jnp.einsum('...dn,...dm->...nm', left, right, precision=HIGH)  52.2 us
    ppermute x12, waiting for transfers between devices, partner(): return lax.ppermute(block, axis, route)  25.2 us
    dot_general x3, matrix products, operate(): local_term = jnp.einsum('lim,nlm->nli', self_blocks, blocks, precision=HIGH)  17.6 us
    ppermute x12, starting transfers between devices, partner(): return lax.ppermute(block, axis, route)  14.1 us
    ppermute x7, starting transfers between devices, passed_along(): lax.ppermute(value, axis, [(source, source + steps) for source in range(f...  12.8 us
  transfers between devices with their start and end apart: 19, of which 8 were waited for; matrix products, arithmetic and copies ran while one was open for 48% of the time, Pallas kernels for 0%

commit v1 on v0

v1 whole, which is shorter than its diff:
```python
import functools
import math

import jax
import jax.numpy as jnp
from jax import lax
from jax.experimental import pallas as pl
from jax.experimental.pallas import tpu as pltpu
from jax.sharding import PartitionSpec as P

ITERS = 3
RIDGE = 8.0
HIGH = lax.Precision.HIGHEST
F32 = jnp.float32
BF16 = jnp.bfloat16


def dot_nn(a, b, precision=None):
    return lax.dot_general(
        a, b, (((1,), (0,)), ((), ())), precision=precision, preferred_element_type=F32
    )


def dot_nt(a, b, precision=None):
    return lax.dot_general(
        a, b, (((1,), (1,)), ((), ())), precision=precision, preferred_element_type=F32
    )


def split2(x):
    hi = x.astype(BF16)
    return hi, (x - hi.astype(F32)).astype(BF16)


def split3(x):
    hi = x.astype(BF16)
    rest = x - hi.astype(F32)
    mid = rest.astype(BF16)
    return hi, mid, (rest - mid.astype(F32)).astype(BF16)


def kernel_block(left, right, scale):
    features = left.shape[0]
    left_t = left.T
    left_sq = jnp.sum(left_t * left_t, axis=1, keepdims=True)
    right_sq = jnp.sum(right * right, axis=0, keepdims=True)
    cross = dot_nn(left_t, right, HIGH)
    return jnp.exp((2.0 * cross - left_sq - right_sq) * (0.5 / features)) * scale


def flipped(value, mask, bits):
    for bit in range(bits):
        weight = 1 << bit
        has = (mask // weight) % 2
        value = value + has * weight * (1 - 2 * ((value // weight) % 2))
    return value


def tree_kernel(
    devices, leaves, rank, slot_ref, le_ref, ls_ref, te_ref, ts_ref, mh_ref, ml_ref, r_ref, t_ref, u_ref
):
    me = lax.axis_index("pts")
    scale = 1.0 / math.sqrt(rank)
    low = leaves.bit_length() - 1
    top = devices.bit_length() - 1
    mh_ref[...] = jnp.zeros_like(mh_ref)
    ml_ref[...] = jnp.zeros_like(ml_ref)

    def local_e(row):
        return le_ref[row * rank : (row + 1) * rank, :]

    def local_s(row):
        return ls_ref[row * rank : (row + 1) * rank, :]

    u_ref[...] = le_ref[0 : leaves * rank, :]
    for depth in range(1, low + 1):
        count = leaves >> depth
        size = (1 << depth) * rank
        if depth < low:
            first = leaves - (leaves >> depth - 1)
            for pair in range(count // 2):
                b = kernel_block(local_s(first + 2 * pair), local_s(first + 2 * pair + 1), scale)
                a0, a1 = 2 * pair * size, (2 * pair + 1) * size
                x, y = u_ref[a0 : a0 + size, :], u_ref[a1 : a1 + size, :]
                p = dot_nn(x, b, HIGH)
                for rows, cols, block in (
                    (a0, a1, dot_nt(p, y, HIGH)),
                    (a1, a0, dot_nt(y, p, HIGH)),
                ):
                    hi, lo = split2(block)
                    mh_ref[rows : rows + size, cols : cols + size] = hi
                    ml_ref[rows : rows + size, cols : cols + size] = lo
            offset = 2 * leaves - 2 * count
            for node in range(count):
                rows = slice(node * size, (node + 1) * size)
                u_ref[rows, :] = dot_nn(u_ref[rows, :], local_e(offset + node), HIGH)
    r_ref[...] = u_ref[...]

    t_ref[...] = jnp.zeros_like(t_ref)

    def slot_of(depth, node):
        return slot_ref[2 * devices - 2 * (devices >> depth) + node]

    def top_row(ref, slot):
        return ref[pl.ds(pl.multiple_of(slot * rank, rank), rank), :]

    chain = None
    seeds = []
    for depth in range(top):
        mine = me // (1 << depth)
        own = slot_of(depth, mine)
        other = slot_of(depth, flipped(mine, 1, 1))
        b = kernel_block(top_row(ts_ref, other), top_row(ts_ref, own), scale)
        seeds.append(b if chain is None else dot_nt(b, chain, HIGH))
        e = top_row(te_ref, own)
        chain = e if chain is None else dot_nn(chain, e, HIGH)
    for depth in range(top - 1, -1, -1):
        mine = me // (1 << depth)
        count = devices >> depth

        def child(step, carry, depth=depth, mine=mine, count=count):
            x = count - 1 - step
            e = top_row(te_ref, slot_of(depth, flipped(mine, x, top - depth)))
            t_ref[x] = dot_nn(e, t_ref[x // 2], HIGH)
            return carry

        if count > 2:
            lax.fori_loop(0, count - 2, child, 0)
        t_ref[1] = seeds[depth]


def main_kernel(
    devices,
    leaves,
    rank,
    columns,
    leaf_size,
    features,
    slots,
    idx_ref,
    wt_ref,
    inv_ref,
    pts_ref,
    next_pts_ref,
    rhs_ref,
    next_rhs_ref,
    basis_ref,
    mh_ref,
    ml_ref,
    r_ref,
    t_ref,
    sol_ref,
    out_ref,
    kh,
    kl,
    bj,
    bd,
    vb,
    sent,
    res,
    along,
    dirn,
    img,
    halo_res,
    halo_along,
    halo_img,
    owed_out,
    owed_in,
    gather,
    g_send,
    g_recv,
    h_send,
    h_recv,
    o_send,
    o_recv,
):
    me = lax.axis_index("pts")
    bits = devices.bit_length() - 1
    following = (me + 1) % devices
    previous = (me + devices - 1) % devices
    near = slots - 1
    n = leaf_size
    barrier = pltpu.get_barrier_semaphore()

    def greet(d, carry):
        pl.semaphore_signal(
            barrier, inc=1, device_id={"pts": (me + d) % devices},
            device_id_type=pl.DeviceIdType.MESH,
        )
        return carry

    lax.fori_loop(1, devices, greet, 0)
    pl.semaphore_wait(barrier, devices - 1)

    def broadcast(slot):
        def post(d, carry):
            pltpu.make_async_remote_copy(
                src_ref=gather.at[slot, me],
                dst_ref=gather.at[slot, me],
                send_sem=g_send.at[slot],
                recv_sem=g_recv.at[slot],
                device_id={"pts": (me + d) % devices},
                device_id_type=pl.DeviceIdType.MESH,
            ).start()
            return carry

        lax.fori_loop(1, devices, post, 0)

    def collect(slot):
        others = gather.at[slot, pl.ds(0, devices - 1)]
        pltpu.make_async_copy(others, others, g_recv.at[slot]).wait()
        pltpu.make_async_copy(others, others, g_send.at[slot]).wait()

    def pair_of(ref, p):
        return jnp.concatenate([ref[2 * p], ref[2 * p + 1]], axis=1)

    def charges_of(ref):
        parts = [dot_nt(pair_of(ref, p), bd[p], HIGH) for p in range(leaves // 2)]
        return jnp.concatenate(parts, axis=1)

    def row_sum(first, second):
        total = first[0] * second[0]
        for l in range(1, leaves):
            total = total + first[l] * second[l]
        return jnp.sum(total, axis=1, keepdims=True)

    def post_message(slot, root, norm, product):
        half = (128 - rank) // 2
        gather[slot, me, :, 0:rank] = root
        gather[slot, me, :, rank : rank + half] = jnp.broadcast_to(norm, (columns, half))
        gather[slot, me, :, rank + half : 128] = jnp.broadcast_to(product, (columns, half))
        broadcast(slot)

    def sums_of(slot):
        total = gather[slot, 0]
        for d in range(1, devices):
            total = total + gather[slot, d]
        half = (128 - rank) // 2
        return total[:, rank : rank + 1], total[:, rank + half : rank + half + 1]

    def potential_of(slot):
        def add(x, total):
            d = flipped(me, x, bits)
            return total + dot_nn(gather[slot, d][:, 0:rank], t_ref[x], HIGH)

        return lax.fori_loop(1, devices, add, jnp.zeros((columns, rank), F32))

    bd[...] = jnp.zeros_like(bd)
    for l in range(leaves):
        odd = l % 2
        bd[l // 2, odd * rank : (odd + 1) * rank, odd * n : (odd + 1) * n] = basis_ref[l]
        res[l] = rhs_ref[:, l * n : (l + 1) * n]
        halo_res[l] = next_rhs_ref[:, l * n : (l + 1) * n]
    charge = charges_of(res)
    norm_local = row_sum(res, res)
    post_message(0, dot_nn(charge, r_ref[...], HIGH), norm_local, norm_local)

    sent[leaves * near] = jnp.zeros((columns, n), F32)

    def stack_right(x, row):
        hi, mid, lo = split3(x)
        nh, nm, nl = split3(-0.5 * jnp.sum(x * x, axis=0, keepdims=True))
        at = lax.broadcasted_iota(jnp.int32, (features, n), 0)
        extra = jnp.where(at < 3, 1.0, 0.0)
        for place, part in ((3, nh), (4, nm), (5, nl)):
            extra = jnp.where(at == place, part.astype(F32), extra)
        bj[row, 0:features, :] = hi
        bj[row, features : 2 * features, :] = mid
        bj[row, 2 * features : 3 * features, :] = lo
        bj[row, 3 * features : 4 * features, :] = extra.astype(BF16)

    def prepare(l, carry):
        at = pl.ds(pl.multiple_of(l * n, n), n)
        stack_right(pts_ref[:, at], l)
        stack_right(next_pts_ref[:, at], leaves + l)
        return carry

    lax.fori_loop(0, leaves, prepare, 0)

    def build(l, carry):
        x = pts_ref[:, pl.ds(pl.multiple_of(l * n, n), n)].T
        hi, mid, lo = split3(x)
        nh, nm, nl = split3(-0.5 * jnp.sum(x * x, axis=1, keepdims=True))
        at = lax.broadcasted_iota(jnp.int32, (n, features), 1)
        extra = jnp.where((at >= 3) & (at < 6), 1.0, 0.0)
        for place, part in ((0, nh), (1, nm), (2, nl)):
            extra = jnp.where(at == place, part.astype(F32), extra)
        left = jnp.concatenate([hi, hi, mid, mid, hi, lo, extra.astype(BF16)], axis=1)
        for k in range(slots):
            m = idx_ref[l * slots + k]
            rh = bj[m, 0:features, :]
            rm = bj[m, features : 2 * features, :]
            rl = bj[m, 2 * features : 3 * features, :]
            rx = bj[m, 3 * features : 4 * features, :]
            right = jnp.concatenate([rh, rm, rh, rm, rl, rh, rx], axis=0)
            block = jnp.exp(dot_nn(left, right) * (1.0 / features)) * wt_ref[l * slots + k]
            hi_part, lo_part = split2(block)
            kh[l * slots + k] = hi_part
            kl[l * slots + k] = lo_part
        return carry

    lax.fori_loop(0, leaves, build, 0)

    collect(0)
    potential = potential_of(0)
    step = norm_now = None
    charge_along = potential_along = None

    for sweep in range(ITERS):
        last = sweep + 1 == ITERS

        def load_field(l, carry):
            vb[l, 0:columns, :], vb[l, columns : 2 * columns, :] = split2(res[l])
            vb[leaves + l, 0:columns, :], vb[leaves + l, columns : 2 * columns, :] = split2(
                halo_res[l]
            )
            return carry

        lax.fori_loop(0, leaves, load_field, 0)

        def transposed(l, carry):
            both = vb[l]
            high = both[0:columns]
            for k in range(near):
                first = dot_nn(both, kh[l * slots + k])
                second = dot_nn(high, kl[l * slots + k])
                sent[l * near + k] = first[0:columns] + first[columns:] + second
            return carry

        lax.fori_loop(0, leaves, transposed, 0)

        for c in range(leaves):
            own = jnp.zeros((columns, n), F32)
            beyond = jnp.zeros((columns, n), F32)
            for l in range(leaves):
                term = sent[inv_ref[l * leaves + c]]
                if l < c:
                    own = own + term
                else:
                    beyond = beyond + term
            img[c] = own + RIDGE * res[c]
            owed_out[c] = beyond
        owed = pltpu.make_async_remote_copy(
            src_ref=owed_out,
            dst_ref=owed_in,
            send_sem=o_send.at[sweep],
            recv_sem=o_recv.at[sweep],
            device_id={"pts": following},
            device_id_type=pl.DeviceIdType.MESH,
        )
        owed.start()

        def forward(l, carry):
            total = jnp.zeros((2 * columns, n), F32)
            low = jnp.zeros((columns, n), F32)
            for k in range(slots):
                both = vb[idx_ref[l * slots + k]]
                total = total + dot_nt(both, kh[l * slots + k])
                low = low + dot_nt(both[0:columns], kl[l * slots + k])
            img[l] = img[l] + (total[0:columns] + total[columns:] + low)
            return carry

        lax.fori_loop(0, leaves, forward, 0)

        chi, clo = split2(charge)
        stacked = jnp.concatenate([chi, clo], axis=0)
        first = dot_nn(stacked, mh_ref[...])
        leaf_potential = first[0:columns] + first[columns:] + dot_nn(chi, ml_ref[...])
        leaf_potential = leaf_potential + dot_nt(potential, r_ref[...], HIGH)
        for p in range(leaves // 2):
            far = dot_nn(leaf_potential[:, 2 * p * rank : 2 * (p + 1) * rank], bd[p], HIGH)
            img[2 * p] = img[2 * p] + far[:, 0:n]
            img[2 * p + 1] = img[2 * p + 1] + far[:, n:]

        owed.wait()
        for l in range(leaves):
            img[l] = img[l] + owed_in[l]

        slot = (sweep + 1) % 2
        halo = None
        norm_local = row_sum(res, res)
        product_local = row_sum(res, img)
        if last:
            charge_img = None
            root = jnp.zeros((columns, rank), F32)
        else:
            halo = pltpu.make_async_remote_copy(
                src_ref=img,
                dst_ref=halo_img.at[sweep],
                send_sem=h_send.at[sweep],
                recv_sem=h_recv.at[sweep],
                device_id={"pts": previous},
                device_id_type=pl.DeviceIdType.MESH,
            )
            halo.start()
            charge_img = charges_of(img)
            root = dot_nn(charge_img, r_ref[...], HIGH)
        post_message(slot, root, norm_local, product_local)
        if not last:
            halo.wait()
        collect(slot)
        norm_next, product = sums_of(slot)
        if sweep == 0:
            step = norm_next / product
        else:
            ratio = norm_next / norm_now
            step = norm_next / (product - ratio * norm_next / step)
        norm_now = norm_next
        if not last:
            potential_img = potential_of(slot)
            if sweep == 0:
                charge_along, potential_along = charge_img, potential_img
            else:
                charge_along = charge_img + ratio * charge_along
                potential_along = potential_img + ratio * potential_along
            charge = charge - step * charge_along
            potential = potential - step * potential_along
        for l in range(leaves):
            at = slice(l * n, (l + 1) * n)
            if sweep == 0:
                d, a = res[l], img[l]
                sol = step * d
            else:
                d = res[l] + ratio * dirn[l]
                a = img[l] + ratio * along[l]
                sol = sol_ref[:, at] + step * d
            sol_ref[:, at] = sol
            r = res[l] - step * a
            if last:
                out_ref[:, at] = r
                continue
            dirn[l], along[l], res[l] = d, a, r
            a = halo_img[sweep, l]
            if sweep > 0:
                a = a + ratio * halo_along[l]
            halo_along[l] = a
            halo_res[l] = halo_res[l] - step * a


def per_device(
    points,
    right_side,
    leaf_basis,
    local_transfer,
    local_skeleton,
    top_transfer,
    top_skeleton,
    node_slot,
    near_leaves,
):
    features = points.shape[0]
    leaves, rank, leaf_size = leaf_basis.shape
    columns = right_side.shape[0]
    near = near_leaves.shape[1]
    slots = near + 1
    devices = lax.axis_size("pts")
    position = lax.axis_index("pts")
    ring = [(source, (source - 1) % devices) for source in range(devices)]
    next_rhs = lax.ppermute(right_side, "pts", ring)
    next_points = lax.ppermute(points, "pts", ring)

    present = near_leaves >= 0
    partner = jnp.where(present, near_leaves - position * leaves, -1)
    ids = jnp.arange(leaves, dtype=jnp.int32)
    index = jnp.concatenate([jnp.maximum(partner, 0), ids[:, None]], axis=1).reshape(-1)
    scale = 1.0 / math.sqrt(leaf_size)
    weight = jnp.concatenate([present, jnp.ones((leaves, 1), bool)], axis=1)
    weight = (weight.astype(F32) * scale).reshape(-1)
    target = jnp.where(ids[:, None] < ids[None, :], ids[None, :], ids[None, :] + leaves)
    match = partner[:, None, :] == target[:, :, None]
    place = ids[:, None] * near + jnp.arange(near, dtype=jnp.int32)[None, :]
    inverse = jnp.min(jnp.where(match, place[:, None, :], leaves * near), axis=2).reshape(-1)

    vmem = pl.BlockSpec(memory_space=pltpu.VMEM)
    smem = pl.BlockSpec(memory_space=pltpu.SMEM)
    inner = leaves * rank
    mh, ml, r, t = pl.pallas_call(
        functools.partial(tree_kernel, devices, leaves, rank),
        out_shape=(
            jax.ShapeDtypeStruct((inner, inner), BF16),
            jax.ShapeDtypeStruct((inner, inner), BF16),
            jax.ShapeDtypeStruct((inner, rank), F32),
            jax.ShapeDtypeStruct((devices, rank, rank), F32),
        ),
        in_specs=[smem] + [vmem] * 4,
        out_specs=(vmem,) * 4,
        scratch_shapes=[pltpu.VMEM((inner, rank), F32)],
        compiler_params=pltpu.CompilerParams(vmem_limit_bytes=48 * 1024 * 1024),
        cost_estimate=pl.CostEstimate(
            flops=20_000_000_000, bytes_accessed=20_000_000, transcendentals=0
        ),
        name="tree",
    )(
        node_slot,
        local_transfer.reshape(-1, rank),
        local_skeleton.reshape(-1, rank),
        top_transfer.reshape(-1, rank),
        top_skeleton.reshape(-1, rank),
    )

    field = (leaves, columns, leaf_size)
    width = leaves * leaf_size
    return pl.pallas_call(
        functools.partial(
            main_kernel, devices, leaves, rank, columns, leaf_size, features, slots
        ),
        out_shape=(jax.ShapeDtypeStruct((columns, width), F32),) * 2,
        in_specs=[smem] * 3 + [vmem] * 9,
        out_specs=(vmem,) * 2,
        scratch_shapes=[
            pltpu.VMEM((leaves * slots, leaf_size, leaf_size), BF16),
            pltpu.VMEM((leaves * slots, leaf_size, leaf_size), BF16),
            pltpu.VMEM((2 * leaves, 4 * features, leaf_size), BF16),
            pltpu.VMEM((leaves // 2, 2 * rank, 2 * leaf_size), F32),
            pltpu.VMEM((2 * leaves, 2 * columns, leaf_size), BF16),
            pltpu.VMEM((leaves * near + 1, columns, leaf_size), F32),
            pltpu.VMEM(field, F32),
            pltpu.VMEM(field, F32),
            pltpu.VMEM(field, F32),
            pltpu.VMEM(field, F32),
            pltpu.VMEM(field, F32),
            pltpu.VMEM(field, F32),
            pltpu.VMEM((ITERS - 1,) + field, F32),
            pltpu.VMEM(field, F32),
            pltpu.VMEM(field, F32),
            pltpu.VMEM((2, devices, columns, 128), F32),
            pltpu.SemaphoreType.DMA((2,)),
            pltpu.SemaphoreType.DMA((2,)),
            pltpu.SemaphoreType.DMA((ITERS,)),
            pltpu.SemaphoreType.DMA((ITERS,)),
            pltpu.SemaphoreType.DMA((ITERS,)),
            pltpu.SemaphoreType.DMA((ITERS,)),
        ],
        compiler_params=pltpu.CompilerParams(
            collective_id=0, has_side_effects=True, vmem_limit_bytes=66 * 1000 * 1000
        ),
        name="gradients",
    )(index, weight, inverse, points, next_points, right_side, next_rhs, leaf_basis, mh, ml, r, t)


def solution(mesh):
    return jax.shard_map(
        per_device,
        mesh=mesh,
        in_specs=(
            P(None, ("groups", "pts")),
            P(None, ("groups", "pts")),
            P(("groups", "pts"), None, None),
            P(("groups", "pts"), None),
            P(("groups", "pts"), None),
            P("groups", None),
            P("groups", None),
            P("groups"),
            P(("groups", "pts"), None),
        ),
        out_specs=(P(None, ("groups", "pts")), P(None, ("groups", "pts"))),
        check_vma=False,
    )
```

time: 528 us -> 159 us (0.30)
  matrix products: 293 us -> 0 us
  Pallas kernels: 0 us -> 140 us
  blocking collectives: 89.9 us -> 0 us
  local copies, waits for them, and re-layouts: 49.3 us -> 11.5 us
  waiting for transfers between devices: 25.2 us -> 0.01 us
  starting transfers between devices: 26.9 us -> 6.17 us
  other arithmetic: 20.5 us -> 0.23 us
  between operations: 17.9 us -> 0.75 us
    dot_general x108 -> x0, matrix products: 293 us -> none  [the longest x3 97 us: operate(): sent = jnp.einsum('lkim,nli->nlkm', cross_blocks, blocks, precision=HIGH)]
    pallas_call x0 -> x2, Pallas kernels: none -> 140 us  [the longest x1 124 us: per_device(): pl.pallas_call(functools.partial(main_kernel, devices, leaves, rank, colu...]
    psum x3 -> x0, blocking collectives: 89.9 us -> none  [joined_sums(): return lax.psum((inner_product(vec, vec), inner_product(vec, image)), 'pts')]
    ppermute x19 -> x2, waiting for transfers between devices: 25.2 us -> 0.01 us  [the longest x1 0.01 us: per_device(): next_rhs = lax.ppermute(right_side, 'pts', ring)]
    ppermute x19 -> x2, starting transfers between devices: 26.9 us -> 6.17 us  [the longest x1 5.5 us: per_device(): next_points = lax.ppermute(points, 'pts', ring)]
    reduce_sum x16 -> x0, other arithmetic: 11.5 us -> none  [the longest x5 7.34 us: kernel_block(): right_sq = jnp.sum(right * right, axis=-2)[..., None, :]]
    slice x16 -> x0, local copies, waits for them, and re-layouts: 10.6 us -> none  [the longest x8 4.27 us: per_device(): transfers.append(lower_e[offset:offset + node_count])]
    gather x4 -> x0, local copies, waits for them, and re-layouts: 10.6 us -> none  [the longest x3 6.26 us: operate(): partner_values = joined_values[:, partner_index] * weights[None, :, :, None]]
  transfers between devices with their start and end apart: 19 -> 2, of which waited for: 8 -> 0; matrix products, arithmetic and copies ran while one was open for 48% -> 4% of each run, Pallas kernels for 0% -> 10%
where the time goes in v1:
time: 159 us; the launch traced here: 158 us
  Pallas kernels  140 us (88%)
  local copies, waits for them, and re-layouts  11.5 us (7%)
  starting transfers between devices  6.17 us (4%)
    pallas_call x1, Pallas kernels, per_device(): pl.pallas_call(functools.partial(main_kernel, devices, leaves, rank, colu...  124 us
    pallas_call x1, Pallas kernels, per_device(): pl.pallas_call(functools.partial(tree_kernel, devices, leaves, rank), out...  15.6 us
    ppermute x1, starting transfers between devices, per_device(): next_points = lax.ppermute(points, 'pts', ring)  5.5 us
    unnamed x12, local copies, waits for them, and re-layouts  4.96 us
  transfers between devices with their start and end apart: 2, of which 0 were waited for; matrix products, arithmetic and copies ran while one was open for 4% of the time, Pallas kernels for 10%

profile of v1, /device:TPU:0, one launch (start us, length us, event | category | flops | bytes accessed | tf_op | source)
XLA Modules:
  0.0 158.3 jit_solution(11803271348494385203)
XLA Ops:
  0.6 0.0 copy-start.3
  0.6 5.5 %collective-permute-start = (f32[64,4096]{1,0:T(8,128)}, f32[64,4096]{1,0:T(8,128)}, u32[]{:S(2)}, u32[]{:S(2)}) collective-permute-start(f32[64,4096]{1,0:T(8,128)} %pts_ref.1), channel_id=1, source_target_pairs={{0,15},{1,0},{2,1},{3,2},{4,3},{5,4},{6,5},{7,6},{8,7},{9,8},{10,9... | collective-permute-start | bytes 3145736 | tf_op jit(solution)/shard_map/ppermute | solution.py:460
  6.1 0.7 collective-permute-start.1
  6.8 1.4 reshape.86.le_ref
  8.2 0.0 copy-start.4
  8.3 0.0 copy-start.2
  8.3 1.4 reshape.88.te_ref
  9.7 0.0 copy-done.3
  9.7 0.4 reshape.89.ts_ref
  10.1 1.1 reshape.87.ls_ref
  11.2 0.0 copy-done.4
  11.3 0.0 copy-done.2
  11.3 15.6 %tree.1 = (bf16[1024,1024]{1,0:T(8,128)(2,1)}, bf16[1024,1024]{1,0:T(8,128)(2,1)}, f32[1024,64]{1,0:T(8,128)S(1)}, f32[16,64,64]{2,1,0:T(8,128)S(1)}) custom-call(s32[30]{0:T(128)S(1)} %copy-done.2, f32[1920,64]{1,0:T(8,128)S(1)} %reshape.86.le_ref, f32[896,64]{1,0:T(8,128)S(1)} %reshape.87.ls_ref, f32[1920,64]{1,0:T(8,128)S(1)} %reshape.88.te_ref, ...), custom_call_target="tpu_custom_call" | custom-call | flops 20000000000 | bytes 20000000 | tf_op jit(solution)/shard_map/tree/pallas_call | solution.py:477
  26.9 0.0 copy-start
  26.9 0.8 copy-done
  27.7 0.0 copy-start.1
  27.7 0.8 copy-done.1
  28.5 0.1 copy.17
  28.5 0.1 iota_add_fusion
  28.6 0.1 select_reduce_fusion
  28.7 0.7 reshape.85.inv_ref
  29.4 0.1 copy.15
  29.5 0.7 reshape.83.idx_ref
  30.2 0.1 copy.16
  30.2 0.7 reshape.84.wt_ref
  30.9 0.0 collective-permute-done.1.next_rhs_ref
  30.9 0.0 collective-permute-done.next_pts_ref
  30.9 124.0 %gradients.1 = (f32[16,4096]{1,0:T(8,128)}, f32[16,4096]{1,0:T(8,128)}) custom-call(s32[144]{0:T(256)} %reshape.83.idx_ref, f32[144]{0:T(256)} %reshape.84.wt_ref, s32[256]{0:T(256)} %reshape.85.inv_ref, f32[64,4096]{1,0:T(8,128)} %pts_ref.1, f32[64,4096]{1,0:T(8,128)} %collective-permute-done.next_pts_ref, f32[16,4096]{1,0:T(8,128)} %rhs_ref.1, ...), custom_call_target="tpu_custom_call" | custom-call | tf_op jit(solution)/shard_map/gradients/pallas_call | solution.py:503
  155.0 1.7 %copy.20 = f32[16,4096]{1,0:T(8,128)} copy(f32[16,4096]{1,0:T(8,128)} %get-tuple-element.14) | data formatting | bytes 524288
  156.6 1.7 %copy.21 = f32[16,4096]{1,0:T(8,128)} copy(f32[16,4096]{1,0:T(8,128)} %get-tuple-element.15) | data formatting | bytes 524288
  (8 shorter events, 0.0 us)
Async XLA Ops:
  0.6 9.1 %copy-start.3 = (f32[30,4096]{1,0:T(8,128)S(1)}, f32[30,4096]{1,0:T(8,128)}, u32[]{:S(2)}) copy-start(f32[30,4096]{1,0:T(8,128)} %param.15) | copy-start | bytes 1474564
  0.6 30.3 %collective-permute-start = (f32[64,4096]{1,0:T(8,128)}, f32[64,4096]{1,0:T(8,128)}, u32[]{:S(2)}, u32[]{:S(2)}) collective-permute-start(f32[64,4096]{1,0:T(8,128)} %pts_ref.1), channel_id=1, source_target_pairs={{0,15},{1,0},{2,1},{3,2},{4,3},{5,4},{6,5},{7,6},{8,7},{9,8},{10,9... | collective-permute-start | bytes 3145736 | tf_op jit(solution)/shard_map/ppermute | solution.py:460
  6.1 24.8 %collective-permute-start.1 = (f32[16,4096]{1,0:T(8,128)}, f32[16,4096]{1,0:T(8,128)}, u32[]{:S(2)}, u32[]{:S(2)}) collective-permute-start(f32[16,4096]{1,0:T(8,128)} %rhs_ref.1), channel_id=1, source_target_pairs={{0,15},{1,0},{2,1},{3,2},{4,3},{5,4},{6,5},{7,6},{8,7},{9,8},{10,9... | collective-permute-start | bytes 786440 | tf_op jit(solution)/shard_map/ppermute | solution.py:459
  8.2 3.0 %copy-start.4 = (s32[16,8]{0,1:T(8,128)S(1)}, s32[16,8]{0,1:T(8,128)}, u32[]{:S(2)}) copy-start(s32[16,8]{0,1:T(8,128)} %param.17) | copy-start | bytes 1540
  8.3 3.0 %copy-start.2 = (s32[30]{0:T(128)S(1)}, s32[30]{0:T(128)}, u32[]{:S(2)}) copy-start(s32[30]{0:T(128)} %slot_ref.1) | copy-start | bytes 364
  26.9 0.8 copy-start
  27.7 0.8 copy-start.1

commit v2 on v1

--- a/solution.py
+++ b/solution.py
@@ -37,6 +37,13 @@
     rest = x - hi.astype(F32)
     mid = rest.astype(BF16)
     return hi, mid, (rest - mid.astype(F32)).astype(BF16)
+
+
+def split_dot(dot, x, hi, lo):
+    rows = x.shape[0]
+    xh, xl = split2(x)
+    first = dot(jnp.concatenate([xh, xl], axis=0), hi)
+    return first[0:rows] + first[rows:] + dot(xh, lo)
 
 
 def kernel_block(left, right, scale):
@@ -57,7 +64,7 @@
 
 
 def tree_kernel(
-    devices, leaves, rank, slot_ref, le_ref, ls_ref, te_ref, ts_ref, mh_ref, ml_ref, r_ref, t_ref, u_ref
+    devices, leaves, rank, slot_ref, le_ref, ls_ref, te_ref, ts_ref, mh_ref, ml_ref, rh_ref, rl_ref, t_ref, u_ref
 ):
     me = lax.axis_index("pts")
     scale = 1.0 / math.sqrt(rank)
@@ -94,7 +101,7 @@
             for node in range(count):
                 rows = slice(node * size, (node + 1) * size)
                 u_ref[rows, :] = dot_nn(u_ref[rows, :], local_e(offset + node), HIGH)
-    r_ref[...] = u_ref[...]
+    rh_ref[...], rl_ref[...] = split2(u_ref[...])
 
     t_ref[...] = jnp.zeros_like(t_ref)
 
@@ -118,14 +125,18 @@
         mine = me // (1 << depth)
         count = devices >> depth
 
-        def child(step, carry, depth=depth, mine=mine, count=count):
-            x = count - 1 - step
-            e = top_row(te_ref, slot_of(depth, flipped(mine, x, top - depth)))
-            t_ref[x] = dot_nn(e, t_ref[x // 2], HIGH)
+        group = min(count, 16)
+
+        def family(step, carry, depth=depth, mine=mine, count=count, group=group):
+            base = count - (step + 1) * group
+            parents = [t_ref[(base + i) // 2] for i in range(group)]
+            for i in range(group):
+                e = top_row(te_ref, slot_of(depth, flipped(mine, base + i, top - depth)))
+                t_ref[base + i] = dot_nn(e, parents[i], HIGH)
             return carry
 
         if count > 2:
-            lax.fori_loop(0, count - 2, child, 0)
+            lax.fori_loop(0, count // group, family, 0)
         t_ref[1] = seeds[depth]
 
 
@@ -147,23 +158,25 @@
     basis_ref,
     mh_ref,
     ml_ref,
-    r_ref,
+    rh_ref,
+    rl_ref,
     t_ref,
     sol_ref,
     out_ref,
     kh,
     kl,
     bj,
-    bd,
+    bdh,
+    bdl,
     vb,
     sent,
     res,
     along,
     dirn,
     img,
-    halo_res,
-    halo_along,
-    halo_img,
+    w,
+    second_along,
+    halo_in,
     owed_out,
     owed_in,
     gather,
@@ -215,7 +228,7 @@
         return jnp.concatenate([ref[2 * p], ref[2 * p + 1]], axis=1)
 
     def charges_of(ref):
-        parts = [dot_nt(pair_of(ref, p), bd[p], HIGH) for p in range(leaves // 2)]
+        parts = [split_dot(dot_nt, pair_of(ref, p), bdh[p], bdl[p]) for p in range(leaves // 2)]
         return jnp.concatenate(parts, axis=1)
 
     def row_sum(first, second):
@@ -239,21 +252,27 @@
         return total[:, rank : rank + 1], total[:, rank + half : rank + half + 1]
 
     def potential_of(slot):
-        def add(x, total):
-            d = flipped(me, x, bits)
-            return total + dot_nn(gather[slot, d][:, 0:rank], t_ref[x], HIGH)
-
-        return lax.fori_loop(1, devices, add, jnp.zeros((columns, rank), F32))
-
-    bd[...] = jnp.zeros_like(bd)
+        group = min(devices, 16)
+
+        def add(step, total):
+            for i in range(group):
+                x = step * group + i
+                d = flipped(me, x, bits)
+                total = total + dot_nn(gather[slot, d][:, 0:rank], t_ref[x], HIGH)
+            return total
+
+        return lax.fori_loop(0, devices // group, add, jnp.zeros((columns, rank), F32))
+
+    bdh[...] = jnp.zeros_like(bdh)
+    bdl[...] = jnp.zeros_like(bdl)
     for l in range(leaves):
         odd = l % 2
-        bd[l // 2, odd * rank : (odd + 1) * rank, odd * n : (odd + 1) * n] = basis_ref[l]
+        rows, cols = slice(odd * rank, (odd + 1) * rank), slice(odd * n, (odd + 1) * n)
+        bdh[l // 2, rows, cols], bdl[l // 2, rows, cols] = split2(basis_ref[l])
         res[l] = rhs_ref[:, l * n : (l + 1) * n]
-        halo_res[l] = next_rhs_ref[:, l * n : (l + 1) * n]
     charge = charges_of(res)
     norm_local = row_sum(res, res)
-    post_message(0, dot_nn(charge, r_ref[...], HIGH), norm_local, norm_local)
+    post_message(0, split_dot(dot_nn, charge, rh_ref[...], rl_ref[...]), norm_local, norm_local)
 
     sent[leaves * near] = jnp.zeros((columns, n), F32)
 
@@ -287,13 +306,13 @@
             extra = jnp.where(at == place, part.astype(F32), extra)
         left = jnp.concatenate([hi, hi, mid, mid, hi, lo, extra.astype(BF16)], axis=1)
         for k in range(slots):
-            m = idx_ref[l * slots + k]
+            m = idx_ref[l, k]
             rh = bj[m, 0:features, :]
             rm = bj[m, features : 2 * features, :]
             rl = bj[m, 2 * features : 3 * features, :]
             rx = bj[m, 3 * features : 4 * features, :]
             right = jnp.concatenate([rh, rm, rh, rm, rl, rh, rx], axis=0)
-            block = jnp.exp(dot_nn(left, right) * (1.0 / features)) * wt_ref[l * slots + k]
+            block = jnp.exp(dot_nn(left, right) * (1.0 / features)) * wt_ref[l, k]
             hi_part, lo_part = split2(block)
             kh[l * slots + k] = hi_part
             kl[l * slots + k] = lo_part
@@ -301,22 +320,17 @@
 
     lax.fori_loop(0, leaves, build, 0)
 
-    collect(0)
-    potential = potential_of(0)
-    step = norm_now = None
-    charge_along = potential_along = None
-
+    halo = None
+    step = ratio = norm_now = None
     for sweep in range(ITERS):
-        last = sweep + 1 == ITERS
-
-        def load_field(l, carry):
-            vb[l, 0:columns, :], vb[l, columns : 2 * columns, :] = split2(res[l])
-            vb[leaves + l, 0:columns, :], vb[leaves + l, columns : 2 * columns, :] = split2(
-                halo_res[l]
-            )
+        slot = sweep % 2
+        field = res if sweep == 0 else w
+
+        def load_own(l, carry):
+            vb[l, 0:columns, :], vb[l, columns : 2 * columns, :] = split2(field[l])
             return carry
 
-        lax.fori_loop(0, leaves, load_field, 0)
+        lax.fori_loop(0, leaves, load_own, 0)
 
         def transposed(l, carry):
             both = vb[l]
@@ -329,16 +343,17 @@
 
         lax.fori_loop(0, leaves, transposed, 0)
 
+        collect(slot)
         for c in range(leaves):
             own = jnp.zeros((columns, n), F32)
             beyond = jnp.zeros((columns, n), F32)
             for l in range(leaves):
-                term = sent[inv_ref[l * leaves + c]]
+                term = sent[inv_ref[l, c]]
                 if l < c:
                     own = own + term
                 else:
                     beyond = beyond + term
-            img[c] = own + RIDGE * res[c]
+            img[c] = own + RIDGE * field[c]
             owed_out[c] = beyond
         owed = pltpu.make_async_remote_copy(
             src_ref=owed_out,
@@ -350,91 +365,86 @@
         )
         owed.start()
 
+        potential = potential_of(slot)
+        chi, clo = split2(charge)
+        first = dot_nn(jnp.concatenate([chi, clo], axis=0), mh_ref[...])
+        leaf_potential = first[0:columns] + first[columns:] + dot_nn(chi, ml_ref[...])
+        leaf_potential = leaf_potential + split_dot(dot_nt, potential, rh_ref[...], rl_ref[...])
+        for p in range(leaves // 2):
+            x = leaf_potential[:, 2 * p * rank : 2 * (p + 1) * rank]
+            far = split_dot(dot_nn, x, bdh[p], bdl[p])
+            img[2 * p] = img[2 * p] + far[:, 0:n]
+            img[2 * p + 1] = img[2 * p + 1] + far[:, n:]
+
+        if halo is not None:
+            halo.wait()
+        for l in range(leaves):
+            x = next_rhs_ref[:, l * n : (l + 1) * n] if sweep == 0 else halo_in[sweep - 1, l]
+            vb[leaves + l, 0:columns, :], vb[leaves + l, columns : 2 * columns, :] = split2(x)
+
         def forward(l, carry):
             total = jnp.zeros((2 * columns, n), F32)
             low = jnp.zeros((columns, n), F32)
             for k in range(slots):
-                both = vb[idx_ref[l * slots + k]]
+                both = vb[idx_ref[l, k]]
                 total = total + dot_nt(both, kh[l * slots + k])
                 low = low + dot_nt(both[0:columns], kl[l * slots + k])
             img[l] = img[l] + (total[0:columns] + total[columns:] + low)
             return carry
 
         lax.fori_loop(0, leaves, forward, 0)
-
-        chi, clo = split2(charge)
-        stacked = jnp.concatenate([chi, clo], axis=0)
-        first = dot_nn(stacked, mh_ref[...])
-        leaf_potential = first[0:columns] + first[columns:] + dot_nn(chi, ml_ref[...])
-        leaf_potential = leaf_potential + dot_nt(potential, r_ref[...], HIGH)
-        for p in range(leaves // 2):
-            far = dot_nn(leaf_potential[:, 2 * p * rank : 2 * (p + 1) * rank], bd[p], HIGH)
-            img[2 * p] = img[2 * p] + far[:, 0:n]
-            img[2 * p + 1] = img[2 * p + 1] + far[:, n:]
-
         owed.wait()
-        for l in range(leaves):
-            img[l] = img[l] + owed_in[l]
+
+        if sweep == 0:
+            for l in range(leaves):
+                w[l] = img[l] + owed_in[l]
+        else:
+            norm_next, product = sums_of(slot)
+            if sweep == 1:
+                step = norm_next / product
+            else:
+                ratio = norm_next / norm_now
+                step = norm_next / (product - ratio * norm_next / step)
+            norm_now = norm_next
+            for l in range(leaves):
+                at = slice(l * n, (l + 1) * n)
+                d, a, z = res[l], w[l], img[l] + owed_in[l]
+                if sweep > 1:
+                    d = d + ratio * dirn[l]
+                    a = a + ratio * along[l]
+                    z = z + ratio * second_along[l]
+                    sol_ref[:, at] = sol_ref[:, at] + step * d
+                else:
+                    sol_ref[:, at] = step * d
+                dirn[l], along[l], second_along[l] = d, a, z
+                res[l] = res[l] - step * a
+                w[l] = w[l] - step * z
 
         slot = (sweep + 1) % 2
-        halo = None
-        norm_local = row_sum(res, res)
-        product_local = row_sum(res, img)
-        if last:
-            charge_img = None
-            root = jnp.zeros((columns, rank), F32)
-        else:
+        root = jnp.zeros((columns, rank), F32)
+        if sweep + 1 < ITERS:
             halo = pltpu.make_async_remote_copy(
-                src_ref=img,
-                dst_ref=halo_img.at[sweep],
+                src_ref=w,
+                dst_ref=halo_in.at[sweep],
                 send_sem=h_send.at[sweep],
                 recv_sem=h_recv.at[sweep],
                 device_id={"pts": previous},
                 device_id_type=pl.DeviceIdType.MESH,
             )
             halo.start()
-            charge_img = charges_of(img)
-            root = dot_nn(charge_img, r_ref[...], HIGH)
-        post_message(slot, root, norm_local, product_local)
-        if not last:
-            halo.wait()
-        collect(slot)
-        norm_next, product = sums_of(slot)
-        if sweep == 0:
-            step = norm_next / product
-        else:
-            ratio = norm_next / norm_now
-            step = norm_next / (product - ratio * norm_next / step)
-        norm_now = norm_next
-        if not last:
-            potential_img = potential_of(slot)
-            if sweep == 0:
-                charge_along, potential_along = charge_img, potential_img
-            else:
-                charge_along = charge_img + ratio * charge_along
-                potential_along = potential_img + ratio * potential_along
-            charge = charge - step * charge_along
-            potential = potential - step * potential_along
-        for l in range(leaves):
-            at = slice(l * n, (l + 1) * n)
-            if sweep == 0:
-                d, a = res[l], img[l]
-                sol = step * d
-            else:
-                d = res[l] + ratio * dirn[l]
-                a = img[l] + ratio * along[l]
-                sol = sol_ref[:, at] + step * d
-            sol_ref[:, at] = sol
-            r = res[l] - step * a
-            if last:
-                out_ref[:, at] = r
-                continue
-            dirn[l], along[l], res[l] = d, a, r
-            a = halo_img[sweep, l]
-            if sweep > 0:
-                a = a + ratio * halo_along[l]
-            halo_along[l] = a
-            halo_res[l] = halo_res[l] - step * a
+            charge = charges_of(w)
+            root = split_dot(dot_nn, charge, rh_ref[...], rl_ref[...])
+        post_message(slot, root, row_sum(res, res), row_sum(res, w))
+
+    slot = ITERS % 2
+    collect(slot)
+    norm_next, product = sums_of(slot)
+    ratio = norm_next / norm_now
+    step = norm_next / (product - ratio * norm_next / step)
+    for l in range(leaves):
+        at = slice(l * n, (l + 1) * n)
+        sol_ref[:, at] = sol_ref[:, at] + step * (res[l] + ratio * dirn[l])
+        out_ref[:, at] = res[l] - step * (w[l] + ratio * along[l])
 
 
 def per_device(
@@ -462,28 +472,29 @@
     present = near_leaves >= 0
     partner = jnp.where(present, near_leaves - position * leaves, -1)
     ids = jnp.arange(leaves, dtype=jnp.int32)
-    index = jnp.concatenate([jnp.maximum(partner, 0), ids[:, None]], axis=1).reshape(-1)
+    index = jnp.concatenate([jnp.maximum(partner, 0), ids[:, None]], axis=1)
     scale = 1.0 / math.sqrt(leaf_size)
     weight = jnp.concatenate([present, jnp.ones((leaves, 1), bool)], axis=1)
-    weight = (weight.astype(F32) * scale).reshape(-1)
+    weight = weight.astype(F32) * scale
     target = jnp.where(ids[:, None] < ids[None, :], ids[None, :], ids[None, :] + leaves)
     match = partner[:, None, :] == target[:, :, None]
     place = ids[:, None] * near + jnp.arange(near, dtype=jnp.int32)[None, :]
-    inverse = jnp.min(jnp.where(match, place[:, None, :], leaves * near), axis=2).reshape(-1)
+    inverse = jnp.min(jnp.where(match, place[:, None, :], leaves * near), axis=2)
 
     vmem = pl.BlockSpec(memory_space=pltpu.VMEM)
     smem = pl.BlockSpec(memory_space=pltpu.SMEM)
     inner = leaves * rank
-    mh, ml, r, t = pl.pallas_call(
+    mh, ml, rh, rl, t = pl.pallas_call(
         functools.partial(tree_kernel, devices, leaves, rank),
         out_shape=(
             jax.ShapeDtypeStruct((inner, inner), BF16),
             jax.ShapeDtypeStruct((inner, inner), BF16),
-            jax.ShapeDtypeStruct((inner, rank), F32),
+            jax.ShapeDtypeStruct((inner, rank), BF16),
+            jax.ShapeDtypeStruct((inner, rank), BF16),
             jax.ShapeDtypeStruct((devices, rank, rank), F32),
         ),
         in_specs=[smem] + [vmem] * 4,
-        out_specs=(vmem,) * 4,
+        out_specs=(vmem,) * 5,
         scratch_shapes=[pltpu.VMEM((inner, rank), F32)],
         compiler_params=pltpu.CompilerParams(vmem_limit_bytes=48 * 1024 * 1024),
         cost_estimate=pl.CostEstimate(
@@ -505,13 +516,14 @@
             main_kernel, devices, leaves, rank, columns, leaf_size, features, slots
         ),
         out_shape=(jax.ShapeDtypeStruct((columns, width), F32),) * 2,
-        in_specs=[smem] * 3 + [vmem] * 9,
+        in_specs=[smem] * 3 + [vmem] * 10,
         out_specs=(vmem,) * 2,
         scratch_shapes=[
             pltpu.VMEM((leaves * slots, leaf_size, leaf_size), BF16),
             pltpu.VMEM((leaves * slots, leaf_size, leaf_size), BF16),
             pltpu.VMEM((2 * leaves, 4 * features, leaf_size), BF16),
-            pltpu.VMEM((leaves // 2, 2 * rank, 2 * leaf_size), F32),
+            pltpu.VMEM((leaves // 2, 2 * rank, 2 * leaf_size), BF16),
+            pltpu.VMEM((leaves // 2, 2 * rank, 2 * leaf_size), BF16),
             pltpu.VMEM((2 * leaves, 2 * columns, leaf_size), BF16),
             pltpu.VMEM((leaves * near + 1, columns, leaf_size), F32),
             pltpu.VMEM(field, F32),
@@ -535,7 +547,7 @@
             collective_id=0, has_side_effects=True, vmem_limit_bytes=66 * 1000 * 1000
         ),
         name="gradients",
-    )(index, weight, inverse, points, next_points, right_side, next_rhs, leaf_basis, mh, ml, r, t)
+    )(index, weight, inverse, points, next_points, right_side, next_rhs, leaf_basis, mh, ml, rh, rl, t)
 
 
 def solution(mesh):

time: 159 us -> 132 us (0.83)
  Pallas kernels: 140 us -> 113 us
  other arithmetic: 0.23 us -> 2.07 us
    pallas_call x1, Pallas kernels: 124 us -> 101 us  [per_device(): pl.pallas_call(functools.partial(main_kernel, devices, leaves, rank, colu...]
    pallas_call x1, Pallas kernels: 15.6 us -> 12.1 us  [per_device(): pl.pallas_call(functools.partial(tree_kernel, devices, leaves, rank), out...]
    reshape x3 -> x0, local copies, waits for them, and re-layouts: 1.96 us -> none  [the longest x1 0.66 us: per_device(): jnp.min(jnp.where(match, place[:, None, :], leaves * near), axis=2)]
    unnamed x12 -> x15, local copies, waits for them, and re-layouts: 4.96 us -> 5.65 us
  transfers between devices with their start and end apart: 2 -> 2, of which waited for: 0 -> 0; matrix products, arithmetic and copies ran while one was open for 4% -> 5% of each run, Pallas kernels for 10% -> 9%
where the time goes in v2:
time: 132 us
  Pallas kernels  113 us (86%)
  local copies, waits for them, and re-layouts  10 us (8%)
  starting transfers between devices  6.17 us (5%)
  other arithmetic  2.07 us (2%)
    pallas_call x1, Pallas kernels, per_device(): pl.pallas_call(functools.partial(main_kernel, devices, leaves, rank, colu...  101 us
    pallas_call x1, Pallas kernels, per_device(): pl.pallas_call(functools.partial(tree_kernel, devices, leaves, rank), out...  12.1 us
    unnamed x15, local copies, waits for them, and re-layouts  5.65 us
    ppermute x1, starting transfers between devices, per_device(): next_points = lax.ppermute(points, 'pts', ring)  5.5 us
  transfers between devices with their start and end apart: 2, of which 0 were waited for; matrix products, arithmetic and copies ran while one was open for 5% of the time, Pallas kernels for 9%

profile of v2, /device:TPU:0, one launch (start us, length us, event | category | flops | bytes accessed | tf_op | source)
XLA Modules:
  0.0 132.1 jit_solution(6605734244948364499)
XLA Ops:
  0.6 0.0 copy-start.4
  0.6 5.5 %collective-permute-start = (f32[64,4096]{1,0:T(8,128)}, f32[64,4096]{1,0:T(8,128)}, u32[]{:S(2)}, u32[]{:S(2)}) collective-permute-start(f32[64,4096]{1,0:T(8,128)} %pts_ref.1), channel_id=1, source_target_pairs={{0,15},{1,0},{2,1},{3,2},{4,3},{5,4},{6,5},{7,6},{8,7},{9,8},{10,9... | collective-permute-start | bytes 3145736 | tf_op jit(solution)/shard_map/ppermute | solution.py:470
  6.1 0.7 collective-permute-start.1
  6.8 1.4 %reshape.74.le_ref = f32[1920,64]{1,0:T(8,128)S(1)} reshape(f32[30,4096]{1,0:T(8,128)} %param.12) | data formatting | bytes 983040 | tf_op jit(solution)/shard_map/reshape | solution.py:506
  8.2 0.0 copy-start.3
  8.3 1.4 %reshape.76.te_ref = f32[1920,64]{1,0:T(8,128)S(1)} reshape(f32[30,4096]{1,0:T(8,128)} %param.14) | data formatting | bytes 983040 | tf_op jit(solution)/shard_map/reshape | solution.py:508
  9.7 0.0 copy-done.4
  9.7 0.4 reshape.77.ts_ref
  10.1 1.1 reshape.75.ls_ref
  11.2 0.1 iota_add_fusion
  11.3 0.0 copy-done.3
  11.3 0.0 copy-start.5
  11.3 12.1 %tree.1 = (bf16[1024,1024]{1,0:T(8,128)(2,1)}, bf16[1024,1024]{1,0:T(8,128)(2,1)}, bf16[1024,64]{1,0:T(8,128)(2,1)S(1)}, bf16[1024,64]{1,0:T(8,128)(2,1)S(1)}, f32[16,64,64]{2,1,0:T(8,128)S(1)}) custom-call(s32[30]{0:T(128)S(1)} %copy-done.3, f32[1920,64]{1,0:T(8,128)S(1)} %reshape.74.le_ref, f32[896,64]{1,0:T(8,128)S(1)} %reshape.75.ls_ref, ...), custom_call_target="tpu_custom_call" | custom-call | flops 20000000000 | bytes 20000000 | tf_op jit(solution)/shard_map/tree/pallas_call | solution.py:487
  23.4 0.0 copy-start
  23.4 0.8 copy-done
  24.2 0.0 copy-start.1
  24.2 0.7 copy-done.1
  24.9 0.0 copy-start.2
  24.9 0.7 copy-done.2
  25.6 0.0 copy-done.5
  25.6 0.1 copy.15
  25.7 0.6 pad_select_fusion.wt_ref
  26.3 0.7 pad_add_fusion.idx_ref
  27.0 0.7 select_reduce_fusion.inv_ref
  27.7 0.0 collective-permute-done.1.next_rhs_ref
  27.7 0.0 collective-permute-done.next_pts_ref
  27.7 101.1 %gradients.1 = (f32[16,4096]{1,0:T(8,128)}, f32[16,4096]{1,0:T(8,128)}) custom-call(s32[16,9]{1,0:T(8,128)} %pad_add_fusion.idx_ref, f32[16,9]{1,0:T(8,128)} %pad_select_fusion.wt_ref, s32[16,16]{1,0:T(8,128)} %select_reduce_fusion.inv_ref, f32[64,4096]{1,0:T(8,128)} %pts_ref.1, f32[64,4096]{1,0:T(8,128)} %collective-permute-done.next_pts_ref, ...), custom_call_target="tpu_custom_call" | custom-call | tf_op jit(solution)/shard_map/gradients/pallas_call | solution.py:514
  128.7 1.7 %copy.19 = f32[16,4096]{1,0:T(8,128)} copy(f32[16,4096]{1,0:T(8,128)} %get-tuple-element.16) | data formatting | bytes 524288
  130.4 1.7 %copy.20 = f32[16,4096]{1,0:T(8,128)} copy(f32[16,4096]{1,0:T(8,128)} %get-tuple-element.17) | data formatting | bytes 524288
  (6 shorter events, 0.0 us)
Async XLA Ops:
  0.6 9.1 %copy-start.4 = (f32[30,4096]{1,0:T(8,128)S(1)}, f32[30,4096]{1,0:T(8,128)}, u32[]{:S(2)}) copy-start(f32[30,4096]{1,0:T(8,128)} %param.15) | copy-start | bytes 1474564
  0.6 27.0 %collective-permute-start = (f32[64,4096]{1,0:T(8,128)}, f32[64,4096]{1,0:T(8,128)}, u32[]{:S(2)}, u32[]{:S(2)}) collective-permute-start(f32[64,4096]{1,0:T(8,128)} %pts_ref.1), channel_id=1, source_target_pairs={{0,15},{1,0},{2,1},{3,2},{4,3},{5,4},{6,5},{7,6},{8,7},{9,8},{10,9... | collective-permute-start | bytes 3145736 | tf_op jit(solution)/shard_map/ppermute | solution.py:470
  6.1 21.5 %collective-permute-start.1 = (f32[16,4096]{1,0:T(8,128)}, f32[16,4096]{1,0:T(8,128)}, u32[]{:S(2)}, u32[]{:S(2)}) collective-permute-start(f32[16,4096]{1,0:T(8,128)} %rhs_ref.1), channel_id=1, source_target_pairs={{0,15},{1,0},{2,1},{3,2},{4,3},{5,4},{6,5},{7,6},{8,7},{9,8},{10,9... | collective-permute-start | bytes 786440 | tf_op jit(solution)/shard_map/ppermute | solution.py:469
  8.2 3.1 %copy-start.3 = (s32[30]{0:T(128)S(1)}, s32[30]{0:T(128)}, u32[]{:S(2)}) copy-start(s32[30]{0:T(128)} %slot_ref.1) | copy-start | bytes 364
  11.3 14.3 %copy-start.5 = (s32[16,8]{0,1:T(8,128)S(1)}, s32[16,8]{0,1:T(8,128)}, u32[]{:S(2)}) copy-start(s32[16,8]{0,1:T(8,128)} %param.17) | copy-start | bytes 1540
  23.4 0.8 copy-start
  24.2 0.7 copy-start.1
  24.9 0.7 copy-start.2
